TPU v7x, 32 devices: a whole 2x2x4 slice. The times are simulated.
32 devices in a mesh: band: 8 (over z, x), mem: 4 (over y, core).
Axes of the slice: x: 2, y: 2, z: 4, core: 2. Of those that a mesh axis runs over, the one named last changes fastest.
Arguments:
- state: float32 [256, 64, 256], P('mem', 'band'), may hold values from -6 to 6
- courant: float32 [2, 64, 256], P(None, 'band'), may hold values from 0.15 to 0.4
- obs_pert: bfloat16 [8, 512, 256], P('band'), may hold values from -8 to 8
- obs_cell: int32 [8, 512], P('band'), may hold values from 0 to 16383, as said below
- block_rows: int32 [8], replicated, may hold values from 64 to 512, as said below
- band_list: int32 [8, 2], P('band'), may hold values from 0 to 7, as said below
Outputs:
- analysis: float32 [256, 64, 256], P('mem', 'band')
Inputs may be any that keep to these rules, and one draw needn't show every extreme that they name: `band_list`: row b holds 2 different block numbers, each one of b - 1, b, b + 1 taken modulo 8. `block_rows`: the first that many rows of a block are live. Some block has exactly 512 in every draw. `obs_cell`: the rows of block j lie in latitude rows j * 8 to (j + 1) * 8 - 1; a cell is numbered latitude row times 256 plus longitude.
All inputs are finite; a program needn't handle non-finite values.
Results may differ from a plain program's by a relative error of at most 0.0045.
Values may be sent and summed in bfloat16 or wider, within the bound.
A program may use at most 64 MiB of HBM per device.

v0:
```python
import jax
import jax.numpy as jnp
from jax import lax
from jax.sharding import PartitionSpec as P

STEPS = 6
LIST = 2
DEGREE = 4


DIFFUSION = 0.05
COEFFS = (1.0, -0.5, 0.375, -0.3125, 0.2734375)


def padded_2(cells, sides, width):
    for axis, dim in sides:
        count = lax.axis_size(axis)
        head = lax.slice_in_dim(cells, 0, width, axis=dim)
        tail = lax.slice_in_dim(cells, cells.shape[dim] - width, cells.shape[dim], axis=dim)
        cells = jnp.concatenate(
            [
                lax.ppermute(tail, axis, [(i, (i + 1) % count) for i in range(count)]),
                cells,
                lax.ppermute(head, axis, [((i + 1) % count, i) for i in range(count)]),
            ],
            axis=dim,
        )
    return cells


def advance(padded, winds):
    centre = padded[:, 1:-1]
    northern = padded[:, :-2]
    southern = padded[:, 2:]
    western = jnp.roll(centre, 1, axis=2)
    eastern = jnp.roll(centre, -1, axis=2)
    saturation = 0.5 + 0.5 * jnp.tanh(centre)
    return (
        centre
        - winds[0][None] * saturation * (centre - northern)
        - winds[1][None] * saturation * (centre - western)
        + DIFFUSION * (northern + southern + eastern + western - 4.0 * centre)
    )


def localization(obs_cells, live_rows, cell_flat, lat_count, lon_count, rows_band, gscale):
    obs_lat = obs_cells // lon_count
    obs_lon = obs_cells % lon_count
    cell_lat = cell_flat // lon_count
    cell_lon = cell_flat % lon_count
    lat_gap = jnp.abs(obs_lat[:, None] - cell_lat[None, :])
    lat_gap = jnp.minimum(lat_gap, lat_count - lat_gap)
    lon_gap = jnp.abs(obs_lon[:, None] - cell_lon[None, :])
    lon_gap = jnp.minimum(lon_gap, lon_count - lon_gap)
    lat_term = lat_gap.astype(jnp.float32) * (1.0 / rows_band)
    lon_term = lon_gap.astype(jnp.float32) * (4.0 / lon_count)
    decay = jnp.exp(-0.5 * (lat_term * lat_term + lon_term * lon_term)) * gscale
    return jnp.where(live_rows[:, None], decay, jnp.zeros_like(decay))


def transform(pert, observed, weight):
    series = pert
    combined = COEFFS[0] * pert
    for power in range(1, DEGREE + 1):
        projected = jnp.dot(
            observed, series.astype(jnp.bfloat16), preferred_element_type=jnp.float32
        )
        scaled = (projected * weight).astype(jnp.bfloat16)
        series = lax.dot_general(
            observed, scaled, (((0,), (0,)), ((), ())), preferred_element_type=jnp.float32
        )
        combined = combined + COEFFS[power] * series
    return combined


def shards(state, courant, obs_pert, obs_cell, block_rows, band_list):
    member_count, band_rows, lon_count = state.shape
    joined = jnp.concatenate([state, courant], axis=0)
    widened = padded_2(joined, (("band", 1),), STEPS)
    tracer = widened[:member_count]
    winds = widened[member_count:]
    for section in range(STEPS):
        inner = tracer.shape[1] - 2
        tracer = advance(tracer, winds[:, section + 1 : section + 1 + inner])
    band_cells = band_rows * lon_count
    columns = lax.all_to_all(
        tracer.reshape(member_count, band_cells), "mem", split_axis=1, concat_axis=0, tiled=True
    )
    members, group_cells = columns.shape
    average = jnp.mean(columns, axis=0, keepdims=True)
    pert = columns - average
    band_index = lax.axis_index("band")
    band_total = lax.axis_size("band")
    mem_index = lax.axis_index("mem")
    block_ids = band_list[0]
    offsets = (block_ids - band_index + 1) % band_total
    near_pert, near_cells = (
        padded_2(obs_pert, (("band", 0),), 1),
        padded_2(obs_cell, (("band", 0),), 1),
    )
    chosen = jnp.stack(
        [
            lax.dynamic_index_in_dim(near_pert, offsets[position], 0, keepdims=False)
            for position in range(LIST)
        ]
    )
    chosen_cells = jnp.stack(
        [
            lax.dynamic_index_in_dim(near_cells, offsets[position], 0, keepdims=False)
            for position in range(LIST)
        ]
    )
    block_count = block_rows.shape[0]
    matches = jnp.arange(block_count, dtype=jnp.int32)[None, :] == block_ids[:, None]
    counts = jnp.sum(
        jnp.where(matches, block_rows[None, :], jnp.zeros_like(block_rows)[None, :]), axis=1
    )
    obs_rows = chosen.shape[1]
    live_rows = (jnp.arange(obs_rows, dtype=jnp.int32)[None, :] < counts[:, None]).reshape(-1)
    observed = chosen.reshape(LIST * obs_rows, members)
    cell_flat = (
        band_index * band_cells + mem_index * group_cells + jnp.arange(group_cells, dtype=jnp.int32)
    )
    gscale = 1.0 / (members + LIST * obs_rows)
    weight = localization(
        chosen_cells.reshape(-1),
        live_rows,
        cell_flat,
        band_rows * band_total,
        lon_count,
        band_rows,
        gscale,
    )
    analysed = average + transform(pert, observed, weight)
    returned = lax.all_to_all(analysed, "mem", split_axis=0, concat_axis=1, tiled=True)
    return returned.reshape(member_count, band_rows, lon_count)


def solution(mesh):
    return jax.shard_map(
        shards,
        mesh=mesh,
        in_specs=(
            P("mem", "band", None),
            P(None, "band", None),
            P("band", None, None),
            P("band", None),
            P(),
            P("band", None),
        ),
        out_specs=P("mem", "band", None),
        check_vma=False,
    )
```

profile of v0, /device:TPU:0, one launch (start us, length us, event | category | flops | bytes accessed | tf_op | source)
XLA Modules:
  0.0 85.0 jit_solution(405076336876510803)
XLA Ops:
  0.0 2.9 %collective-permute-start.4 = (s32[1,512]{1,0:T(1,128)}, s32[1,512]{1,0:T(1,128)S(1)}, u32[]{:S(2)}, u32[]{:S(2)}) collective-permute-start(s32[1,512]{1,0:T(1,128)} %param.9), channel_id=1, source_target_pairs={{0,4},{4,8},{8,12},{12,16},{16,20},{20,24},{24,28},{28,0},{1,5},{5... | collective-permute-start | bytes 6152 | tf_op jit(solution)/shard_map/ppermute | solution.py:22
  2.9 3.0 %collective-permute-start.5 = (s32[1,512]{1,0:T(1,128)}, s32[1,512]{1,0:T(1,128)S(1)}, u32[]{:S(2)}, u32[]{:S(2)}) collective-permute-start(s32[1,512]{1,0:T(1,128)} %param.9), channel_id=1, source_target_pairs={{4,0},{8,4},{12,8},{16,12},{20,16},{24,20},{28,24},{0,28},{5,1},{9... | collective-permute-start | bytes 6152 | tf_op jit(solution)/shard_map/ppermute | solution.py:24
  6.0 4.7 %collective-permute-start.3 = (bf16[1,512,256]{2,1,0:T(8,128)(2,1)}, bf16[1,512,256]{2,1,0:T(8,128)(2,1)S(1)}, u32[]{:S(2)}, u32[]{:S(2)}) collective-permute-start(bf16[1,512,256]{2,1,0:T(8,128)(2,1)} %param.8), channel_id=1, source_target_pairs={{4,0},{8,4},{12,8},{16,12},{20,16},{24,20},{28,24},{0,28},{5,1},{9... | collective-permute-start | bytes 786440 | tf_op jit(solution)/shard_map/ppermute | solution.py:24
  10.7 1.1 %constant_dynamic-update-slice_fusion.1 = f32[66,8,256]{2,1,0:T(8,128)S(1)} fusion(f32[64,8,256]{2,1,0:T(8,128)} %param.6), kind=kLoop, calls=%fused_computation.88 | loop fusion | bytes 1048576
  11.8 0.8 constant_dynamic-update-slice_fusion
  12.6 0.1 fusion.109
  12.7 0.1 copy.32
  12.8 0.1 collective-permute-start.1
  12.9 0.6 fusion.110
  13.5 0.2 fusion.67
  13.7 0.1 iota_compare_fusion
  16.2 0.1 copy.31
  17.5 2.0 %collective-permute-start = (f32[66,6,256]{2,0,1:T(8,128)S(1)}, f32[66,6,256]{2,0,1:T(8,128)S(1)}, u32[]{:S(2)}, u32[]{:S(2)}) collective-permute-start(f32[66,6,256]{2,0,1:T(8,128)S(1)} %copy.31), channel_id=1, source_target_pairs={{0,4},{4,8},{8,12},{12,16},{16,20},{20,24},{24,28},{28,0},{1,5},{5... | collective-permute-start | bytes 1216520 | tf_op jit(solution)/shard_map/ppermute | solution.py:22
  19.6 8.5 %collective-permute-done.2 = bf16[1,512,256]{2,1,0:T(8,128)(2,1)} collective-permute-done((bf16[1,512,256]{2,1,0:T(8,128)(2,1)}, bf16[1,512,256]{2,1,0:T(8,128)(2,1)}, u32[]{:S(2)}, u32[]{:S(2)}) %collective-permute-start.2) | collective-permute-done | bytes 262176 | tf_op jit(solution)/shard_map/ppermute | solution.py:22
  28.1 1.0 %constant_dynamic-update-slice_fusion.4 = bf16[3,512,256]{2,1,0:T(8,128)(2,1)S(1)} fusion(bf16[1,512,256]{2,1,0:T(8,128)(2,1)} %collective-permute-done.2), kind=kLoop, calls=%fused_computation.91 | loop fusion | bytes 524288
  29.1 9.5 %collective-permute-done.1 = f32[66,6,256]{2,0,1:T(8,128)S(1)} collective-permute-done((f32[66,6,256]{2,0,1:T(8,128)S(1)}, f32[66,6,256]{2,0,1:T(8,128)S(1)}, u32[]{:S(2)}, u32[]{:S(2)}) %collective-permute-start.1) | collective-permute-done | bytes 405536 | tf_op jit(solution)/shard_map/ppermute | solution.py:24
  38.5 0.1 copy.34
  38.7 0.1 copy.33
  38.9 0.2 pad_maximum_fusion
  39.2 0.3 fusion.97
  39.5 0.6 fusion.98
  40.0 1.4 %fusion.15 = f32[64,18,256]{2,1,0:T(8,128)S(1)} fusion(f32[66,20,256]{2,1,0:T(8,128)S(1)} %pad_maximum_fusion, f32[64,18,1]{2,1,0:T(8,128)S(1)} %get-tuple-element.16, f32[64,18,255]{2,1,0:T(8,128)S(1)} %get-tuple-element.18, f32[64,18,255]{2,1,0:T(8,128)S(1)} %get-tuple-element.17, f32[64,18,1]{2,1,0:T(8,128)S(1)} %get-tuple-element.15, ...), kind=kLoop, calls=%fused_computation.23 | loop fusion | flops 5603328 | bytes 7114752 | tf_op jit(solution)/shard_map/add | solution.py:39
  41.5 0.2 fusion.99
  41.7 0.4 fusion.100
  42.1 1.0 %fusion.42 = f32[64,16,256]{2,1,0:T(8,128)S(1)} fusion(f32[64,18,256]{2,1,0:T(8,128)S(1)} %fusion.15, f32[64,16,1]{2,1,0:T(8,128)S(1)} %get-tuple-element.20, f32[64,16,255]{2,1,0:T(8,128)S(1)} %get-tuple-element.22, f32[64,16,255]{2,1,0:T(8,128)S(1)} %get-tuple-element.21, f32[64,16,1]{2,1,0:T(8,128)S(1)} %get-tuple-element.19, ...), kind=kLoop, calls=%fused_computation.55 | loop fusion | flops 4980736 | bytes 6324224 | tf_op jit(solution)/shard_map/add | solution.py:39
  43.1 0.2 fusion.107
  43.3 0.4 fusion.108
  43.7 1.0 %fusion.37 = f32[64,14,256]{2,1,0:T(8,128)S(1)} fusion(f32[64,16,256]{2,1,0:T(8,128)S(1)} %fusion.42, f32[64,14,1]{2,1,0:T(8,128)S(1)} %get-tuple-element.36, f32[64,14,255]{2,1,0:T(8,128)S(1)} %get-tuple-element.38, f32[64,14,255]{2,1,0:T(8,128)S(1)} %get-tuple-element.37, f32[64,14,1]{2,1,0:T(8,128)S(1)} %get-tuple-element.35, ...), kind=kLoop, calls=%fused_computation.49 | loop fusion | flops 4358144 | bytes 5533696 | tf_op jit(solution)/shard_map/add | solution.py:39
  44.8 0.2 fusion.105
  45.0 0.4 fusion.106
  45.4 1.0 %fusion.32 = f32[64,12,256]{2,1,0:T(8,128)S(1)} fusion(f32[64,14,256]{2,1,0:T(8,128)S(1)} %fusion.37, f32[64,12,1]{2,1,0:T(8,128)S(1)} %get-tuple-element.32, f32[64,12,255]{2,1,0:T(8,128)S(1)} %get-tuple-element.34, f32[64,12,255]{2,1,0:T(8,128)S(1)} %get-tuple-element.33, f32[64,12,1]{2,1,0:T(8,128)S(1)} %get-tuple-element.31, ...), kind=kLoop, calls=%fused_computation.43 | loop fusion | flops 3735552 | bytes 4743168 | tf_op jit(solution)/shard_map/add | solution.py:39
  46.4 0.2 fusion.103
  46.6 0.4 fusion.104
  47.0 1.0 %fusion.27 = f32[64,10,256]{2,1,0:T(8,128)S(1)} fusion(f32[64,12,256]{2,1,0:T(8,128)S(1)} %fusion.32, f32[64,10,1]{2,1,0:T(8,128)S(1)} %get-tuple-element.28, f32[64,10,255]{2,1,0:T(8,128)S(1)} %get-tuple-element.30, f32[64,10,255]{2,1,0:T(8,128)S(1)} %get-tuple-element.29, f32[64,10,1]{2,1,0:T(8,128)S(1)} %get-tuple-element.27, ...), kind=kLoop, calls=%fused_computation.37 | loop fusion | flops 3112960 | bytes 3952640 | tf_op jit(solution)/shard_map/add | solution.py:39
  48.0 0.1 fusion.101
  48.1 0.2 fusion.102
  48.4 0.5 fusion.51
  48.9 0.2 all_to_all.26
  49.1 1.0 %copy.35 = f32[64,4,512]{2,0,1:T(8,128)} copy(f32[64,4,512]{2,1,0:T(4,128)S(1)} %all_to_all.26) | data formatting | bytes 1048576 | tf_op jit(solution)/shard_map/all_to_all | solution.py:86
  50.1 3.7 %all-to-all-start = ((f32[64,4,512]{2,0,1:T(8,128)}), f32[64,4,512]{2,0,1:T(8,128)S(1)}, u32[]{:S(2)}, u32[]{:S(2)}) async-start(f32[64,4,512]{2,0,1:T(8,128)} %copy.35), calls=%async_computation | async-start | bytes 1048576 | tf_op jit(solution)/shard_map/all_to_all | solution.py:86
  53.9 8.4 %all-to-all-done = f32[64,4,512]{2,0,1:T(8,128)S(1)} async-done(((f32[64,4,512]{2,0,1:T(8,128)}), f32[64,4,512]{2,0,1:T(8,128)S(1)}, u32[]{:S(2)}, u32[]{:S(2)}) %all-to-all-start) | async-done | bytes 524320 | tf_op jit(solution)/shard_map/all_to_all | solution.py:86
  62.5 2.5 %fusion.16 = f32[256,512]{1,0:T(8,128)S(1)} fusion(bf16[1024,256]{1,0:T(8,128)(2,1)S(1)} %bitcast.59, bf16[256,512]{1,0:T(8,128)(2,1)S(1)} %bitcast.64, s32[512]{0:T(512)S(1)} %get-tuple-element.53, s32[1024]{0:T(1024)S(1)} %get-tuple-element.48, s32[512]{0:T(512)S(1)} %get-tuple-element.54, s32[1024]{0:T(1024)S(1)} %get-tuple-element.47, ...), kind=kOutput, calls=%fused_computation.25 | convolution fusion | flops 547356672 | bytes 1324032 | tf_op jit(solution)/shard_map/dot_general | solution.py:69
  64.9 2.5 %fusion.17 = f32[256,512]{1,0:T(8,128)S(1)} fusion(bf16[1024,256]{1,0:T(8,128)(2,1)S(1)} %bitcast.60, s32[512]{0:T(512)S(1)} %get-tuple-element.53, s32[1024]{0:T(1024)S(1)} %get-tuple-element.48, s32[512]{0:T(512)S(1)} %get-tuple-element.54, s32[1024]{0:T(1024)S(1)} %get-tuple-element.47, pred[1024]{0:T(1024)(128)(4,1)S(1)} %lt.54, f32[256,512]{1,0:T(8,128)S(1)} %fusion.16), kind=kOutput, calls=%fused_computation.26 | convolution fusion | flops 547487744 | bytes 1586176 | tf_op jit(solution)/shard_map/dot_general | solution.py:69
  67.4 2.5 %fusion.54 = (f32[256,512]{1,0:T(8,128)S(1)}, bf16[256,512]{1,0:T(8,128)(2,1)S(1)}) fusion(f32[64,4,512]{2,0,1:T(8,128)S(1)} %all-to-all-done, f32[256,512]{1,0:T(8,128)S(1)} %fusion.17, f32[256,512]{1,0:T(8,128)S(1)} %fusion.16, f32[512]{0:T(512)S(1)} %broadcast_multiply_fusion, bf16[1024,256]{1,0:T(8,128)(2,1)S(1)} %bitcast.61, ...), kind=kOutput, calls=%fused_computation.71 | convolution fusion | flops 548536320 | bytes 2898944 | tf_op jit(solution)/shard_map/dot_general | solution.py:69
  69.9 2.5 %fusion.22 = f32[256,512]{1,0:T(8,128)S(1)} fusion(f32[256,512]{1,0:T(8,128)S(1)} %get-tuple-element.51, bf16[1024,256]{1,0:T(8,128)(2,1)S(1)} %bitcast.62, s32[512]{0:T(512)S(1)} %get-tuple-element.53, s32[1024]{0:T(1024)S(1)} %get-tuple-element.48, s32[512]{0:T(512)S(1)} %get-tuple-element.54, s32[1024]{0:T(1024)S(1)} %get-tuple-element.47, ...), kind=kOutput, calls=%fused_computation.31 | convolution fusion | flops 547749888 | bytes 1850368 | tf_op jit(solution)/shard_map/dot_general | solution.py:69
  72.4 11.2 %all_to_all.35 = f32[4,64,512]{2,1,0:T(8,128)S(1)} all-to-all(f32[4,64,512]{2,1,0:T(8,128)S(1)} %bitcast.63), channel_id=1, replica_groups=mesh['band'=8,'mem'=4] {'mem'}, dimensions={0} | all-to-all | bytes 1048576 | tf_op jit(solution)/shard_map/all_to_all | solution.py:135
  83.6 0.3 copy.36
  84.0 1.0 %reshape.128 = f32[64,8,256]{2,1,0:T(8,128)} reshape(f32[64,4,512]{2,1,0:T(4,128)S(1)} %copy.36) | data formatting | bytes 1048576 | tf_op jit(solution)/shard_map/reshape | solution.py:136
  (36 shorter events, 0.4 us)
Async XLA Ops:
  0.0 17.5 %collective-permute-start.4 = (s32[1,512]{1,0:T(1,128)}, s32[1,512]{1,0:T(1,128)S(1)}, u32[]{:S(2)}, u32[]{:S(2)}) collective-permute-start(s32[1,512]{1,0:T(1,128)} %param.9), channel_id=1, source_target_pairs={{0,4},{4,8},{8,12},{12,16},{16,20},{20,24},{24,28},{28,0},{1,5},{5... | collective-permute-start | bytes 6152 | tf_op jit(solution)/shard_map/ppermute | solution.py:22
  2.9 16.6 %collective-permute-start.5 = (s32[1,512]{1,0:T(1,128)}, s32[1,512]{1,0:T(1,128)S(1)}, u32[]{:S(2)}, u32[]{:S(2)}) collective-permute-start(s32[1,512]{1,0:T(1,128)} %param.9), channel_id=1, source_target_pairs={{4,0},{8,4},{12,8},{16,12},{20,16},{24,20},{28,24},{0,28},{5,1},{9... | collective-permute-start | bytes 6152 | tf_op jit(solution)/shard_map/ppermute | solution.py:24
  6.0 22.1 %collective-permute-start.2 = (bf16[1,512,256]{2,1,0:T(8,128)(2,1)}, bf16[1,512,256]{2,1,0:T(8,128)(2,1)}, u32[]{:S(2)}, u32[]{:S(2)}) collective-permute-start(bf16[1,512,256]{2,1,0:T(8,128)(2,1)} %param.8), channel_id=1, source_target_pairs={{0,4},{4,8},{8,12},{12,16},{16,20},{20,24},{24,28},{28,0},{1,5},{5... | collective-permute-start | bytes 786440 | tf_op jit(solution)/shard_map/ppermute | solution.py:22
  6.0 47.8 %collective-permute-start.3 = (bf16[1,512,256]{2,1,0:T(8,128)(2,1)}, bf16[1,512,256]{2,1,0:T(8,128)(2,1)S(1)}, u32[]{:S(2)}, u32[]{:S(2)}) collective-permute-start(bf16[1,512,256]{2,1,0:T(8,128)(2,1)} %param.8), channel_id=1, source_target_pairs={{4,0},{8,4},{12,8},{16,12},{20,16},{24,20},{28,24},{0,28},{5,1},{9... | collective-permute-start | bytes 786440 | tf_op jit(solution)/shard_map/ppermute | solution.py:24
  11.8 1.1 %copy-start.1 = (f32[2,8,256]{2,1,0:T(8,128)S(1)}, f32[2,8,256]{2,1,0:T(8,128)}, u32[]{:S(2)}) copy-start(f32[2,8,256]{2,1,0:T(8,128)} %param.7) | copy-start | bytes 49156
  11.8 1.1 %copy-start.3 = (s32[1,2]{1,0:T(1,128)S(1)}, s32[1,2]{1,0:T(1,128)}, u32[]{:S(2)}) copy-start(s32[1,2]{1,0:T(1,128)} %param.11) | copy-start | bytes 28
  11.8 1.7 %copy-start.4 = (s32[8]{0:T(128)S(1)}, s32[8]{0:T(128)}, u32[]{:S(2)}) copy-start(s32[8]{0:T(128)} %param.10) | copy-start | bytes 100
  12.6 7.0 %copy-start.2 = (s32[1,512]{1,0:T(1,128)S(1)}, s32[1,512]{1,0:T(1,128)}, u32[]{:S(2)}) copy-start(s32[1,512]{1,0:T(1,128)} %param.9) | copy-start | bytes 6148
  12.8 25.7 %collective-permute-start.1 = (f32[66,6,256]{2,0,1:T(8,128)S(1)}, f32[66,6,256]{2,0,1:T(8,128)S(1)}, u32[]{:S(2)}, u32[]{:S(2)}) collective-permute-start(f32[66,6,256]{2,0,1:T(8,128)S(1)} %copy.32), channel_id=1, source_target_pairs={{4,0},{8,4},{12,8},{16,12},{20,16},{24,20},{28,24},{0,28},{5,1},{9... | collective-permute-start | bytes 1216520 | tf_op jit(solution)/shard_map/ppermute | solution.py:24
  17.5 21.2 %collective-permute-start = (f32[66,6,256]{2,0,1:T(8,128)S(1)}, f32[66,6,256]{2,0,1:T(8,128)S(1)}, u32[]{:S(2)}, u32[]{:S(2)}) collective-permute-start(f32[66,6,256]{2,0,1:T(8,128)S(1)} %copy.31), channel_id=1, source_target_pairs={{0,4},{4,8},{8,12},{12,16},{16,20},{20,24},{24,28},{28,0},{1,5},{5... | collective-permute-start | bytes 1216520 | tf_op jit(solution)/shard_map/ppermute | solution.py:22
  48.8 4.9 %copy-start = (bf16[1,512,256]{2,1,0:T(8,128)(2,1)S(1)}, bf16[1,512,256]{2,1,0:T(8,128)(2,1)}, u32[]{:S(2)}) copy-start(bf16[1,512,256]{2,1,0:T(8,128)(2,1)} %param.8) | copy-start | bytes 786436
  50.1 12.3 %all-to-all-start = ((f32[64,4,512]{2,0,1:T(8,128)}), f32[64,4,512]{2,0,1:T(8,128)S(1)}, u32[]{:S(2)}, u32[]{:S(2)}) async-start(f32[64,4,512]{2,0,1:T(8,128)} %copy.35), calls=%async_computation | async-start | bytes 1048576 | tf_op jit(solution)/shard_map/all_to_all | solution.py:86
where the time goes:
time: 85.3 us; the launch traced here: 85 us
  waiting for transfers between devices  26.4 us (31%)
  starting transfers between devices  16.4 us (19%)
  blocking collectives  11.2 us (13%)
  local copies, waits for them, and re-layouts  10.3 us (12%)
  matrix products  9.87 us (12%)
  other arithmetic  6.72 us (8%)
  between operations  4.02 us (5%)
    all_to_all x1, blocking collectives, shards(): lax.all_to_all(analysed, 'mem', split_axis=0, concat_axis=1, tiled=True)  11.2 us
    dot_general x4, matrix products, transform(): lax.dot_general(observed, scaled, (((0,), (0,)), ((), ())), preferred_ele...  9.87 us
    ppermute x3, waiting for transfers between devices, padded_2(): lax.ppermute(head, axis, [((i + 1) % count, i) for i in range(count)])  9.46 us
    ppermute x3, waiting for transfers between devices, padded_2(): lax.ppermute(tail, axis, [(i, (i + 1) % count) for i in range(count)])  8.49 us
    all_to_all x1, waiting for transfers between devices, shards(): lax.all_to_all(tracer.reshape(member_count, band_cells), 'mem', split_axi...  8.45 us
    ppermute x3, starting transfers between devices, padded_2(): lax.ppermute(head, axis, [((i + 1) % count, i) for i in range(count)])  7.82 us
    add x6, other arithmetic, advance(): centre - winds[0][None] * saturation * (centre - northern)  5.96 us
    ppermute x3, starting transfers between devices, padded_2(): lax.ppermute(tail, axis, [(i, (i + 1) % count) for i in range(count)])  4.97 us
  transfers between devices with their start and end apart: 7, of which 3 were waited for; matrix products, arithmetic and copies ran while one was open for 18% of the time, Pallas kernels for 0%

commit v1 on v0

v1 whole, which is shorter than its diff:
```python
import functools

import jax
import jax.numpy as jnp
from jax import lax
from jax.experimental import pallas as pl
from jax.experimental.pallas import tpu as pltpu
from jax.sharding import PartitionSpec as P

STEPS = 6
LIST = 2
DEGREE = 4
DIFFUSION = 0.05
COEFFS = (1.0, -0.5, 0.375, -0.3125, 0.2734375)
CHUNK = 16
SUB = 8
LANES = 128
MESH = pl.DeviceIdType.MESH


def kernel(
    dims,
    state, courant, cells_in, rows_in, list_in, obs,
    out,
    near, near_cells, near_t, weight,
    halo_send, halo_recv, aux_send, aux_recv, halo, wind,
    adv, ref_send, ref_recv, group_send, group_recv, back_send, back_recv, series, total,
    obs_s, obs_r, cell_s, cell_r, spread_s, spread_r, aux_s, aux_r, halo_s, halo_r,
    ref_s, ref_r, group_s, group_r, back_s, back_r, own_sem,
):
    n_band, n_mem, local, band_rows, lon, obs_rows, halves = dims
    chunks = local // CHUNK
    group = band_rows * lon // n_mem
    width = group // halves
    part = obs_rows // n_mem
    members = local * n_mem
    near_winds = STEPS - 1
    b = lax.axis_index("band")
    m = lax.axis_index("mem")
    bands = (lax.rem(b + n_band - 1, n_band), lax.rem(b + 1, n_band))
    peers = [lax.rem(m + k, n_mem) for k in range(n_mem)]

    barrier = pltpu.get_barrier_semaphore()
    for d in range(2):
        pl.semaphore_signal(barrier, inc=1, device_id={"band": bands[d], "mem": m}, device_id_type=MESH)
    for k in range(1, n_mem):
        pl.semaphore_signal(barrier, inc=1, device_id={"band": b, "mem": peers[k]}, device_id_type=MESH)
    pl.semaphore_wait(barrier, 2 + n_mem - 1)

    def to_band(d, src, dst, ssem, rsem):
        return pltpu.make_async_remote_copy(
            src_ref=src, dst_ref=dst, send_sem=ssem, recv_sem=rsem,
            device_id={"band": bands[d], "mem": m}, device_id_type=MESH,
        )

    def to_peer(k, src, dst, ssem, rsem):
        return pltpu.make_async_remote_copy(
            src_ref=src, dst_ref=dst, send_sem=ssem, recv_sem=rsem,
            device_id={"band": b, "mem": peers[k]}, device_id_type=MESH,
        )

    slots = (2, 0)
    mine = pl.ds(pl.multiple_of(m * part, part), part)

    def obs_copy(d):
        return to_band(d, obs.at[0, mine], near.at[slots[d], mine], obs_s.at[d], obs_r.at[d])

    def cell_copy(d):
        return to_band(d, cells_in, near_cells.at[slots[d]], cell_s.at[d], cell_r.at[d])

    def spread_copy(d, k):
        block = near.at[slots[d], mine]
        return to_peer(k, block, block, spread_s.at[d, k], spread_r.at[d, k])

    def aux_copy(d):
        return to_band(d, aux_send.at[d], aux_recv.at[d], aux_s.at[d], aux_r.at[d])

    def halo_copy(d, c):
        return to_band(d, halo_send.at[d, c], halo_recv.at[d, c], halo_s.at[d, c], halo_r.at[d, c])

    def ref_copy(k):
        if k == 0:
            return pltpu.make_async_copy(ref_send.at[m], ref_recv.at[m], ref_s.at[0])
        return to_peer(k, ref_send.at[peers[k]], ref_recv.at[m], ref_s.at[k], ref_r.at[k])

    def group_copy(c, k):
        if k == 0:
            return pltpu.make_async_copy(group_send.at[m, c], group_recv.at[m, c], group_s.at[c, 0])
        return to_peer(k, group_send.at[peers[k], c], group_recv.at[m, c], group_s.at[c, k], group_r.at[c, k])

    def back_copy(h, k):
        if k == 0:
            return pltpu.make_async_copy(back_send.at[h, m], back_recv.at[h, m], back_s.at[h, 0])
        return to_peer(k, back_send.at[h, peers[k]], back_recv.at[h, m], back_s.at[h, k], back_r.at[h, k])

    for d in range(2):
        cell_copy(d).start()
        obs_copy(d).start()
    own_obs = pltpu.make_async_copy(obs.at[0], near.at[1], own_sem)
    own_obs.start()
    near_cells[1] = cells_in[...]

    @pl.loop(0, local // SUB)
    def _(block):
        span = pl.ds(pl.multiple_of(block * SUB, SUB), SUB)
        adv[:, span] = jnp.swapaxes(state[span], 0, 1)

    def outer_rows(d):
        return range(STEPS) if d == 0 else range(band_rows - STEPS, band_rows)

    base = []
    for row in range(band_rows):
        base.append(jnp.sum(adv[row], axis=0, keepdims=True) * (1.0 / local))
    for d in range(2):
        rows = list(outer_rows(d))
        kept = rows[:near_winds] if d == 0 else rows[STEPS - near_winds:]
        for i, row in enumerate(kept):
            aux_send[d, i : i + 1] = courant[0, row : row + 1]
            aux_send[d, near_winds + i : near_winds + i + 1] = courant[1, row : row + 1]
        for i, row in enumerate(rows):
            aux_send[d, 2 * near_winds + i : 2 * near_winds + i + 1] = base[row]
        aux_copy(d).start()

    @pl.loop(0, chunks)
    def _(c):
        full = pl.ds(pl.multiple_of(c * CHUNK, CHUNK), CHUNK)
        for row in range(band_rows):
            both = (adv[row, full] - base[row]).astype(jnp.bfloat16)
            for d in range(2):
                rows = list(outer_rows(d))
                if row in rows:
                    halo_send[d, c, rows.index(row)] = both
        for d in range(2):
            halo_copy(d, c).start()

    for d in range(2):
        obs_copy(d).wait_recv()
        for k in range(1, n_mem):
            spread_copy(d, k).start()
    for d in range(2):
        cell_copy(d).wait_recv()

    ids = [list_in[0, t] for t in range(LIST)]
    offs = [lax.min(lax.rem(ids[t] - b + 1 + n_band, n_band), 2) for t in range(LIST)]
    gscale = 1.0 / (members + LIST * obs_rows)
    nlat = n_band * band_rows
    for t in range(LIST):
        count = rows_in[ids[t]]
        flat = near_cells[offs[t]]
        lat = lax.div(flat, jnp.int32(lon))
        obs_lon = (flat - lat * lon).astype(jnp.float32)
        obs_lat = lat.astype(jnp.float32)
        for piece in range(obs_rows // LANES):
            span = slice(piece * LANES, (piece + 1) * LANES)
            lat_c = jnp.transpose(jnp.broadcast_to(obs_lat[:, span], (LANES, LANES)))
            lon_c = jnp.transpose(jnp.broadcast_to(obs_lon[:, span], (LANES, LANES)))
            live = lax.broadcasted_iota(jnp.int32, (LANES, LANES), 0) + piece * LANES < count
            for block in range(group // LANES):
                first = m * group + block * LANES
                row = first // lon
                cell_lat = (b * band_rows + row).astype(jnp.float32)
                cell_lon = (first - row * lon).astype(jnp.float32) + lax.broadcasted_iota(
                    jnp.int32, (LANES, LANES), 1
                ).astype(jnp.float32)
                lat_gap = jnp.abs(lat_c - cell_lat)
                lat_gap = jnp.minimum(lat_gap, nlat - lat_gap)
                lon_gap = jnp.abs(lon_c - cell_lon)
                lon_gap = jnp.minimum(lon_gap, lon - lon_gap)
                lat_term = lat_gap * (1.0 / band_rows)
                lon_term = lon_gap * (4.0 / lon)
                decay = jnp.exp(-0.5 * (lat_term * lat_term + lon_term * lon_term)) * gscale
                weight[t, span, block * LANES : (block + 1) * LANES] = jnp.where(
                    live, decay, jnp.zeros_like(decay)
                )

    for d in range(2):
        aux_copy(d).wait_recv()
    for part_at in range(2):
        lead = near_winds * part_at
        for i in range(near_winds):
            wind[part_at, i] = jnp.broadcast_to(0.5 * aux_recv[1, lead + i : lead + i + 1], (SUB, lon))
            wind[part_at, near_winds + band_rows + i] = jnp.broadcast_to(
                0.5 * aux_recv[0, lead + i : lead + i + 1], (SUB, lon)
            )
        for i in range(band_rows):
            wind[part_at, near_winds + i] = jnp.broadcast_to(0.5 * courant[part_at, i : i + 1], (SUB, lon))

    def advect(c):
        for d in range(2):
            halo_copy(d, c).wait_recv()
        for d in range(2):
            for i in range(STEPS):
                at = 2 * near_winds + i
                halo[1 - d, i] = halo_recv[d, c, i].astype(jnp.float32) + aux_recv[d, at : at + 1]

        @pl.loop(0, CHUNK // SUB)
        def _(s):
            span = pl.ds(pl.multiple_of(s * SUB, SUB), SUB)
            q = [halo[0, i, span] for i in range(STEPS)]
            full = pl.ds(pl.multiple_of(c * CHUNK + s * SUB, SUB), SUB)
            q += [adv[row, full] for row in range(band_rows)]
            q += [halo[1, i, span] for i in range(STEPS)]
            for step in range(STEPS):
                new = []
                for i in range(1, len(q) - 1):
                    now, north, south = q[i], q[i - 1], q[i + 1]
                    west = pltpu.roll(now, 1, 1)
                    east = pltpu.roll(now, lon - 1, 1)
                    at = i - 1 + step
                    rise = wind[0, at] * (now - north) + wind[1, at] * (now - west)
                    near4 = (north + south) + (east + west)
                    new.append(
                        (1.0 - 4.0 * DIFFUSION) * now + DIFFUSION * near4 - (1.0 + jnp.tanh(now)) * rise
                    )
                q = new
            for row in range(band_rows):
                adv[row, full] = q[row]

    def pieces():
        for row in range(band_rows):
            for lane in range(0, lon, LANES):
                cell = row * lon + lane
                yield row, slice(lane, lane + LANES), cell // group, cell % group

    def regroup(c):
        full = pl.ds(pl.multiple_of(c * CHUNK, CHUNK), CHUNK)
        for row, lanes, g, at in pieces():
            diff = adv[row, full, lanes] - ref_send[g, :, at : at + LANES]
            group_send[g, c, :, at : at + LANES] = diff.astype(jnp.bfloat16)
        for k in range(n_mem):
            group_copy(c, k).start()

    advect(0)
    for row, lanes, g, at in pieces():
        ref_send[g, :, at : at + LANES] = jnp.mean(adv[row, :CHUNK, lanes], axis=0, keepdims=True)
    for k in range(n_mem):
        ref_copy(k).start()
    regroup(0)

    @pl.loop(1, chunks)
    def _(c):
        advect(c)
        regroup(c)

    own_obs.wait()
    for d in range(2):
        for k in range(1, n_mem):
            spread_copy(d, k).wait_recv()
    for t in range(LIST):
        near_t[t] = jnp.transpose(near[offs[t]])

    for k in range(n_mem):
        copies = [ref_copy(k)] + [group_copy(c, k) for c in range(chunks)]
        for copy in copies:
            copy.wait() if k == 0 else copy.wait_recv()
    average = jnp.zeros((1, group), jnp.float32)
    for j in range(n_mem):
        added = jnp.zeros((CHUNK, group), jnp.float32)
        for c in range(chunks):
            added = added + group_recv[j, c].astype(jnp.float32)
        average = average + jnp.sum(added, axis=0, keepdims=True) + local * ref_recv[j]
    average = average * (1.0 / members)
    for j in range(n_mem):
        shift = ref_recv[j] - average
        for c in range(chunks):
            start = j * local + c * CHUNK
            pert = group_recv[j, c].astype(jnp.float32) + shift
            series[start : start + CHUNK] = pert.astype(jnp.bfloat16)

    for h in range(halves):
        lanes = slice(h * width, (h + 1) * width)
        for power in range(1, DEGREE + 1):
            held = series[:, lanes]
            result = None
            for t in range(LIST):
                projected = jnp.dot(near[offs[t]], held, preferred_element_type=jnp.float32)
                scaled = (projected * weight[t, :, lanes]).astype(jnp.bfloat16)
                term = jnp.dot(near_t[t], scaled, preferred_element_type=jnp.float32)
                result = term if result is None else result + term
            if power < DEGREE:
                series[:, lanes] = result.astype(jnp.bfloat16)
            if power == 1:
                total[...] = COEFFS[power] * result
            elif power < DEGREE:
                total[...] += COEFFS[power] * result
            else:
                last = (total[...] + COEFFS[power] * result).astype(jnp.bfloat16)
                for j in range(n_mem):
                    back_send[h, j] = last[j * local : (j + 1) * local]
        for k in range(n_mem):
            back_copy(h, k).start()

    for h in range(halves):
        for k in range(n_mem):
            copy = back_copy(h, k)
            copy.wait() if k == 0 else copy.wait_recv()
        for row, lanes, g, at in pieces():
            if at // width != h:
                continue
            off = at - h * width
            adv[row, :, lanes] += back_recv[h, g, :, off : off + LANES].astype(jnp.float32)

    @pl.loop(0, local // SUB)
    def _(block):
        span = pl.ds(pl.multiple_of(block * SUB, SUB), SUB)
        out[span] = jnp.swapaxes(adv[:, span], 0, 1)

    for d in range(2):
        cell_copy(d).wait_send()
        obs_copy(d).wait_send()
        aux_copy(d).wait_send()
        for c in range(chunks):
            halo_copy(d, c).wait_send()
        for k in range(1, n_mem):
            spread_copy(d, k).wait_send()
    for k in range(1, n_mem):
        ref_copy(k).wait_send()
        for c in range(chunks):
            group_copy(c, k).wait_send()
        for h in range(halves):
            back_copy(h, k).wait_send()


def shards(state, courant, obs_pert, obs_cell, block_rows, band_list):
    local, band_rows, lon = state.shape
    n_band = lax.axis_size("band")
    n_mem = lax.axis_size("mem")
    obs_rows, members = obs_pert.shape[1:]
    group = band_rows * lon // n_mem
    halves = 2 if group >= 4 * LANES else 1
    width = group // halves
    chunks = local // CHUNK
    bf16, f32 = jnp.bfloat16, jnp.float32
    dma = pltpu.SemaphoreType.DMA
    vmem = pl.BlockSpec(memory_space=pltpu.VMEM)
    smem = pl.BlockSpec(memory_space=pltpu.SMEM)
    return pl.pallas_call(
        functools.partial(kernel, (n_band, n_mem, local, band_rows, lon, obs_rows, halves)),
        out_shape=jax.ShapeDtypeStruct(state.shape, f32),
        in_specs=[vmem, vmem, vmem, smem, smem, pl.BlockSpec(memory_space=pl.ANY)],
        out_specs=vmem,
        scratch_shapes=[
            pltpu.VMEM((3, obs_rows, members), bf16),
            pltpu.VMEM((3, 1, obs_rows), jnp.int32),
            pltpu.VMEM((LIST, members, obs_rows), bf16),
            pltpu.VMEM((LIST, obs_rows, group), f32),
            pltpu.VMEM((2, chunks, STEPS, CHUNK, lon), bf16),
            pltpu.VMEM((2, chunks, STEPS, CHUNK, lon), bf16),
            pltpu.VMEM((2, 16, lon), f32),
            pltpu.VMEM((2, 16, lon), f32),
            pltpu.VMEM((2, STEPS, CHUNK, lon), f32),
            pltpu.VMEM((2, band_rows + 2 * (STEPS - 1), SUB, lon), f32),
            pltpu.VMEM((band_rows, local, lon), f32),
            pltpu.VMEM((n_mem, 1, group), f32),
            pltpu.VMEM((n_mem, 1, group), f32),
            pltpu.VMEM((n_mem, chunks, CHUNK, group), bf16),
            pltpu.VMEM((n_mem, chunks, CHUNK, group), bf16),
            pltpu.VMEM((halves, n_mem, local, width), bf16),
            pltpu.VMEM((halves, n_mem, local, width), bf16),
            pltpu.VMEM((members, group), bf16),
            pltpu.VMEM((members, width), f32),
            dma((2,)), dma((2,)), dma((2,)), dma((2,)),
            dma((2, n_mem)), dma((2, n_mem)),
            dma((2,)), dma((2,)),
            dma((2, chunks)), dma((2, chunks)),
            dma((n_mem,)), dma((n_mem,)),
            dma((chunks, n_mem)), dma((chunks, n_mem)),
            dma((halves, n_mem)), dma((halves, n_mem)),
            dma(()),
        ],
        compiler_params=pltpu.CompilerParams(
            collective_id=0, has_side_effects=True, vmem_limit_bytes=40 * 1024 * 1024
        ),
    )(state, courant, obs_cell, block_rows, band_list, obs_pert)


def solution(mesh):
    return jax.shard_map(
        shards,
        mesh=mesh,
        in_specs=(
            P("mem", "band", None),
            P(None, "band", None),
            P("band", None, None),
            P("band", None),
            P(),
            P("band", None),
        ),
        out_specs=P("mem", "band", None),
        check_vma=False,
    )
```

time: 85.3 us -> 38.6 us (0.45)
  Pallas kernels: 0 us -> 32.8 us
  waiting for transfers between devices: 26.4 us -> 0 us
  starting transfers between devices: 16.4 us -> 0 us
  blocking collectives: 11.2 us -> 0 us
  matrix products: 9.87 us -> 0 us
  other arithmetic: 6.72 us -> 0 us
  local copies, waits for them, and re-layouts: 10.3 us -> 5.49 us
  between operations: 4.02 us -> 0.02 us
    pallas_call x0 -> x1, Pallas kernels: none -> 32.8 us  [shards(): pl.pallas_call(functools.partial(kernel, (n_band, n_mem, local, band_rows...]
    ppermute x6 -> x0, waiting for transfers between devices: 17.9 us -> none  [the longest x3 9.46 us: padded_2(): lax.ppermute(head, axis, [((i + 1) % count, i) for i in range(count)])]
    ppermute x6 -> x0, starting transfers between devices: 12.8 us -> none  [the longest x3 7.82 us: padded_2(): lax.ppermute(head, axis, [((i + 1) % count, i) for i in range(count)])]
    all_to_all x1 -> x0, blocking collectives: 11.2 us -> none  [shards(): lax.all_to_all(analysed, 'mem', split_axis=0, concat_axis=1, tiled=True)]
    dot_general x4 -> x0, matrix products: 9.87 us -> none  [transform(): lax.dot_general(observed, scaled, (((0,), (0,)), ((), ())), preferred_ele...]
    all_to_all x1 -> x0, waiting for transfers between devices: 8.45 us -> none  [shards(): lax.all_to_all(tracer.reshape(member_count, band_cells), 'mem', split_axi...]
    add x6 -> x0, other arithmetic: 5.96 us -> none  [advance(): centre - winds[0][None] * saturation * (centre - northern)]
    slice x16 -> x0, local copies, waits for them, and re-layouts: 4.5 us -> none  [the longest x12 3.62 us: advance(): western = jnp.roll(centre, 1, axis=2)]
  transfers between devices with their start and end apart: 7 -> 0, of which waited for: 3 -> 0; matrix products, arithmetic and copies ran while one was open for 18% -> 0% of each run, Pallas kernels for 0% -> 0%
where the time goes in v1:
time: 38.6 us; the launch traced here: 38.3 us
  Pallas kernels  32.8 us (85%)
  local copies, waits for them, and re-layouts  5.49 us (14%)
    pallas_call x1, Pallas kernels, shards(): pl.pallas_call(functools.partial(kernel, (n_band, n_mem, local, band_rows...  32.8 us
    unnamed x13, local copies, waits for them, and re-layouts  5.49 us

profile of v1, /device:TPU:0, one launch (start us, length us, event | category | flops | bytes accessed | tf_op | source)
XLA Modules:
  0.0 38.3 jit_solution(17420560455739953774)
XLA Ops:
  0.0 0.0 copy-start
  0.0 1.0 %copy-done = f32[64,8,256]{2,1,0:T(8,128)S(1)} copy-done((f32[64,8,256]{2,1,0:T(8,128)S(1)}, f32[64,8,256]{2,1,0:T(8,128)}, u32[]{:S(2)}) %copy-start) | copy-done | bytes 524312
  1.0 0.0 copy-start.1
  1.0 0.9 %copy-done.1 = bf16[1,512,256]{2,1,0:T(8,128)(2,1)S(1)} copy-done((bf16[1,512,256]{2,1,0:T(8,128)(2,1)S(1)}, bf16[1,512,256]{2,1,0:T(8,128)(2,1)}, u32[]{:S(2)}) %copy-start.1) | copy-done | bytes 262168
  2.0 0.0 copy-start.2
  2.0 0.7 %copy-done.2 = f32[2,8,256]{2,1,0:T(8,128)S(1)} copy-done((f32[2,8,256]{2,1,0:T(8,128)S(1)}, f32[2,8,256]{2,1,0:T(8,128)}, u32[]{:S(2)}) %copy-start.2) | copy-done | bytes 16408
  2.7 0.0 copy-start.3
  2.7 0.7 %copy-done.3 = s32[1,512]{1,0:T(1,128)S(1)} copy-done((s32[1,512]{1,0:T(1,128)S(1)}, s32[1,512]{1,0:T(1,128)}, u32[]{:S(2)}) %copy-start.3) | copy-done | bytes 2072
  3.4 0.0 copy-start.4
  3.4 0.7 %copy-done.4 = s32[8]{0:T(128)S(1)} copy-done((s32[8]{0:T(128)S(1)}, s32[8]{0:T(128)}, u32[]{:S(2)}) %copy-start.4) | copy-done | bytes 56
  4.0 0.0 copy-start.5
  4.1 0.7 %copy-done.5 = s32[1,2]{1,0:T(1,128)S(1)} copy-done((s32[1,2]{1,0:T(1,128)S(1)}, s32[1,2]{1,0:T(1,128)}, u32[]{:S(2)}) %copy-start.5) | copy-done | bytes 32
  4.7 32.8 %shard_map.64 = f32[64,8,256]{2,1,0:T(8,128)S(1)} custom-call(f32[64,8,256]{2,1,0:T(8,128)S(1)} %copy-done, f32[2,8,256]{2,1,0:T(8,128)S(1)} %copy-done.2, s32[1,512]{1,0:T(1,128)S(1)} %copy-done.3, s32[8]{0:T(128)S(1)} %copy-done.4, s32[1,2]{1,0:T(1,128)S(1)} %copy-done.5, bf16[1,512,256]{2,1,0:T(8,128)(2,1)S(1)} %copy-done.1), custom_call_target="tpu_custom_call" | custom-call | tf_op jit(solution)/shard_map/pallas_call | solution.py:337
  37.5 0.8 %copy.8 = f32[64,8,256]{2,1,0:T(8,128)} copy(f32[64,8,256]{2,1,0:T(8,128)S(1)} %shard_map.64) | data formatting | bytes 1048576
Async XLA Ops:
  0.0 1.0 %copy-start = (f32[64,8,256]{2,1,0:T(8,128)S(1)}, f32[64,8,256]{2,1,0:T(8,128)}, u32[]{:S(2)}) copy-start(f32[64,8,256]{2,1,0:T(8,128)} %state.1) | copy-start | bytes 1572868
  1.0 0.9 %copy-start.1 = (bf16[1,512,256]{2,1,0:T(8,128)(2,1)S(1)}, bf16[1,512,256]{2,1,0:T(8,128)(2,1)}, u32[]{:S(2)}) copy-start(bf16[1,512,256]{2,1,0:T(8,128)(2,1)} %obs.1) | copy-start | bytes 786436
  2.0 0.7 %copy-start.2 = (f32[2,8,256]{2,1,0:T(8,128)S(1)}, f32[2,8,256]{2,1,0:T(8,128)}, u32[]{:S(2)}) copy-start(f32[2,8,256]{2,1,0:T(8,128)} %courant.1) | copy-start | bytes 49156
  2.7 0.7 %copy-start.3 = (s32[1,512]{1,0:T(1,128)S(1)}, s32[1,512]{1,0:T(1,128)}, u32[]{:S(2)}) copy-start(s32[1,512]{1,0:T(1,128)} %cells_in.1) | copy-start | bytes 6148
  3.4 0.7 %copy-start.4 = (s32[8]{0:T(128)S(1)}, s32[8]{0:T(128)}, u32[]{:S(2)}) copy-start(s32[8]{0:T(128)} %rows_in.1) | copy-start | bytes 100
  4.0 0.7 %copy-start.5 = (s32[1,2]{1,0:T(1,128)S(1)}, s32[1,2]{1,0:T(1,128)}, u32[]{:S(2)}) copy-start(s32[1,2]{1,0:T(1,128)} %list_in.1) | copy-start | bytes 28

commit v2 on v1

--- a/solution.py
+++ b/solution.py
@@ -20,13 +20,14 @@
 
 def kernel(
     dims,
-    state, courant, cells_in, rows_in, list_in, obs,
+    state_in, courant_in, cells_in, rows_list, list_list, obs,
     out,
+    state, courant, rows_in, list_in,
     near, near_cells, near_t, weight,
     halo_send, halo_recv, aux_send, aux_recv, halo, wind,
     adv, ref_send, ref_recv, group_send, group_recv, back_send, back_recv, series, total,
     obs_s, obs_r, cell_s, cell_r, spread_s, spread_r, aux_s, aux_r, halo_s, halo_r,
-    ref_s, ref_r, group_s, group_r, back_s, back_r, own_sem,
+    ref_s, ref_r, group_s, group_r, back_s, back_r, own_sem, out_sem,
 ):
     n_band, n_mem, local, band_rows, lon, obs_rows, halves = dims
     chunks = local // CHUNK
@@ -38,8 +39,26 @@
     b = lax.axis_index("band")
     m = lax.axis_index("mem")
     bands = (lax.rem(b + n_band - 1, n_band), lax.rem(b + 1, n_band))
-    peers = [lax.rem(m + k, n_mem) for k in range(n_mem)]
-
+    chip, core = m // 2, m % 2
+    chips = [lax.rem(chip + k, n_mem // 2) for k in range(n_mem // 2)]
+    peers = [chips[k // 2] * 2 + lax.rem(core + k % 2, 2) for k in range(n_mem)]
+    far_first = list(range(n_mem))[::-1]
+
+    loads = [
+        pltpu.make_async_copy(src, dst, own_sem.at[i])
+        for i, (src, dst) in enumerate(
+            (
+                (state_in, state),
+                (courant_in, courant),
+                (cells_in, near_cells.at[1]),
+                (rows_list, rows_in),
+                (list_list, list_in),
+                (obs.at[0], near.at[1]),
+            )
+        )
+    ]
+    for load in loads:
+        load.start()
     barrier = pltpu.get_barrier_semaphore()
     for d in range(2):
         pl.semaphore_signal(barrier, inc=1, device_id={"band": bands[d], "mem": m}, device_id_type=MESH)
@@ -59,6 +78,10 @@
             device_id={"band": b, "mem": peers[k]}, device_id_type=MESH,
         )
 
+    def out_copy(block):
+        span = pl.ds(pl.multiple_of(block * SUB, SUB), SUB)
+        return pltpu.make_async_copy(state.at[span], out.at[span], out_sem.at[block])
+
     slots = (2, 0)
     mine = pl.ds(pl.multiple_of(m * part, part), part)
 
@@ -89,16 +112,16 @@
         return to_peer(k, group_send.at[peers[k], c], group_recv.at[m, c], group_s.at[c, k], group_r.at[c, k])
 
     def back_copy(h, k):
+        src = back_send.at[h, peers[k]]
         if k == 0:
-            return pltpu.make_async_copy(back_send.at[h, m], back_recv.at[h, m], back_s.at[h, 0])
-        return to_peer(k, back_send.at[h, peers[k]], back_recv.at[h, m], back_s.at[h, k], back_r.at[h, k])
+            return pltpu.make_async_copy(src, back_recv.at[h, m], back_s.at[h, 0])
+        return to_peer(k, src, back_recv.at[h, m], back_s.at[h, k], back_r.at[h, k])
 
     for d in range(2):
         cell_copy(d).start()
         obs_copy(d).start()
-    own_obs = pltpu.make_async_copy(obs.at[0], near.at[1], own_sem)
-    own_obs.start()
-    near_cells[1] = cells_in[...]
+    for load in loads[:2]:
+        load.wait()
 
     @pl.loop(0, local // SUB)
     def _(block):
@@ -135,10 +158,13 @@
 
     for d in range(2):
         obs_copy(d).wait_recv()
-        for k in range(1, n_mem):
+        for k in far_first[:-1]:
             spread_copy(d, k).start()
     for d in range(2):
         cell_copy(d).wait_recv()
+
+    for load in loads[2:5]:
+        load.wait()
 
     ids = [list_in[0, t] for t in range(LIST)]
     offs = [lax.min(lax.rem(ids[t] - b + 1 + n_band, n_band), 2) for t in range(LIST)]
@@ -227,7 +253,7 @@
         for row, lanes, g, at in pieces():
             diff = adv[row, full, lanes] - ref_send[g, :, at : at + LANES]
             group_send[g, c, :, at : at + LANES] = diff.astype(jnp.bfloat16)
-        for k in range(n_mem):
+        for k in far_first:
             group_copy(c, k).start()
 
     advect(0)
@@ -242,7 +268,7 @@
         advect(c)
         regroup(c)
 
-    own_obs.wait()
+    loads[5].wait()
     for d in range(2):
         for k in range(1, n_mem):
             spread_copy(d, k).wait_recv()
@@ -267,28 +293,34 @@
             pert = group_recv[j, c].astype(jnp.float32) + shift
             series[start : start + CHUNK] = pert.astype(jnp.bfloat16)
 
+    def scaled(t, lanes):
+        projected = jnp.dot(near[offs[t]], series[:, lanes], preferred_element_type=jnp.float32)
+        return (projected * weight[t, :, lanes]).astype(jnp.bfloat16)
+
+    for power in range(1, DEGREE):
+        result = None
+        for t in range(LIST):
+            term = jnp.dot(near_t[t], scaled(t, slice(0, group)), preferred_element_type=jnp.float32)
+            result = term if result is None else result + term
+        series[...] = result.astype(jnp.bfloat16)
+        if power == 1:
+            total[...] = COEFFS[power] * result
+        else:
+            total[...] += COEFFS[power] * result
     for h in range(halves):
         lanes = slice(h * width, (h + 1) * width)
-        for power in range(1, DEGREE + 1):
-            held = series[:, lanes]
+        last = [scaled(t, lanes) for t in range(LIST)]
+        for at in reversed(range(n_mem // 2)):
+            rows = pl.ds(pl.multiple_of(chips[at] * (2 * local), 2 * local), 2 * local)
             result = None
             for t in range(LIST):
-                projected = jnp.dot(near[offs[t]], held, preferred_element_type=jnp.float32)
-                scaled = (projected * weight[t, :, lanes]).astype(jnp.bfloat16)
-                term = jnp.dot(near_t[t], scaled, preferred_element_type=jnp.float32)
+                term = jnp.dot(near_t[t, rows], last[t], preferred_element_type=jnp.float32)
                 result = term if result is None else result + term
-            if power < DEGREE:
-                series[:, lanes] = result.astype(jnp.bfloat16)
-            if power == 1:
-                total[...] = COEFFS[power] * result
-            elif power < DEGREE:
-                total[...] += COEFFS[power] * result
-            else:
-                last = (total[...] + COEFFS[power] * result).astype(jnp.bfloat16)
-                for j in range(n_mem):
-                    back_send[h, j] = last[j * local : (j + 1) * local]
-        for k in range(n_mem):
-            back_copy(h, k).start()
+            result = (total[rows, lanes] + COEFFS[DEGREE] * result).astype(jnp.bfloat16)
+            for j in range(2):
+                back_send[h, chips[at] * 2 + j] = result[j * local : (j + 1) * local]
+            for k in (2 * at + 1, 2 * at):
+                back_copy(h, k).start()
 
     for h in range(halves):
         for k in range(n_mem):
@@ -303,7 +335,12 @@
     @pl.loop(0, local // SUB)
     def _(block):
         span = pl.ds(pl.multiple_of(block * SUB, SUB), SUB)
-        out[span] = jnp.swapaxes(adv[:, span], 0, 1)
+        state[span] = jnp.swapaxes(adv[:, span], 0, 1)
+        out_copy(block).start()
+
+    @pl.loop(0, local // SUB)
+    def _(block):
+        out_copy(block).wait()
 
     for d in range(2):
         cell_copy(d).wait_send()
@@ -332,14 +369,16 @@
     chunks = local // CHUNK
     bf16, f32 = jnp.bfloat16, jnp.float32
     dma = pltpu.SemaphoreType.DMA
-    vmem = pl.BlockSpec(memory_space=pltpu.VMEM)
-    smem = pl.BlockSpec(memory_space=pltpu.SMEM)
     return pl.pallas_call(
         functools.partial(kernel, (n_band, n_mem, local, band_rows, lon, obs_rows, halves)),
         out_shape=jax.ShapeDtypeStruct(state.shape, f32),
-        in_specs=[vmem, vmem, vmem, smem, smem, pl.BlockSpec(memory_space=pl.ANY)],
-        out_specs=vmem,
+        in_specs=[pl.BlockSpec(memory_space=pltpu.HBM)] * 6,
+        out_specs=pl.BlockSpec(memory_space=pltpu.HBM),
         scratch_shapes=[
+            pltpu.VMEM(state.shape, f32),
+            pltpu.VMEM(courant.shape, f32),
+            pltpu.SMEM(block_rows.shape, jnp.int32),
+            pltpu.SMEM(band_list.shape, jnp.int32),
             pltpu.VMEM((3, obs_rows, members), bf16),
             pltpu.VMEM((3, 1, obs_rows), jnp.int32),
             pltpu.VMEM((LIST, members, obs_rows), bf16),
@@ -358,7 +397,7 @@
             pltpu.VMEM((halves, n_mem, local, width), bf16),
             pltpu.VMEM((halves, n_mem, local, width), bf16),
             pltpu.VMEM((members, group), bf16),
-            pltpu.VMEM((members, width), f32),
+            pltpu.VMEM((members, group), f32),
             dma((2,)), dma((2,)), dma((2,)), dma((2,)),
             dma((2, n_mem)), dma((2, n_mem)),
             dma((2,)), dma((2,)),
@@ -366,10 +405,11 @@
             dma((n_mem,)), dma((n_mem,)),
             dma((chunks, n_mem)), dma((chunks, n_mem)),
             dma((halves, n_mem)), dma((halves, n_mem)),
-            dma(()),
+            dma((6,)),
+            dma((local // SUB,)),
         ],
         compiler_params=pltpu.CompilerParams(
-            collective_id=0, has_side_effects=True, vmem_limit_bytes=40 * 1024 * 1024
+            collective_id=0, has_side_effects=True, vmem_limit_bytes=62 * 1024 * 1024
         ),
     )(state, courant, obs_cell, block_rows, band_list, obs_pert)
 

time: 38.6 us -> 33.7 us (0.87)
  local copies, waits for them, and re-layouts: 5.49 us -> 1.87 us
  Pallas kernels: 32.8 us -> 31.7 us
    unnamed x13 -> x1, local copies, waits for them, and re-layouts: 5.49 us -> 1.87 us
    pallas_call x1, Pallas kernels: 32.8 us -> 31.7 us  [shards(): pl.pallas_call(functools.partial(kernel, (n_band, n_mem, local, band_rows...]
where the time goes in v2:
time: 33.7 us; the launch traced here: 33.6 us
  Pallas kernels  31.7 us (94%)
  local copies, waits for them, and re-layouts  1.87 us (6%)
    pallas_call x1, Pallas kernels, shards(): pl.pallas_call(functools.partial(kernel, (n_band, n_mem, local, band_rows...  31.7 us
    unnamed x1, local copies, waits for them, and re-layouts  1.87 us

profile of v2, /device:TPU:0, one launch (start us, length us, event | category | flops | bytes accessed | tf_op | source)
XLA Modules:
  0.0 33.6 jit_solution(6517474652918330702)
XLA Ops:
  0.0 31.7 %shard_map.64 = f32[64,8,256]{2,1,0:T(8,128)} custom-call(f32[64,8,256]{2,1,0:T(8,128)} %state_in.1, f32[2,8,256]{2,1,0:T(8,128)} %courant_in.1, s32[1,512]{1,0:T(1,128)} %cells_in.1, s32[8]{0:T(128)} %rows_list.1, s32[1,2]{1,0:T(1,128)} %list_list.1, bf16[1,512,256]{2,1,0:T(8,128)(2,1)} %obs.1), custom_call_target="tpu_custom_call" | custom-call | tf_op jit(solution)/shard_map/pallas_call | solution.py:372
  31.7 1.9 %copy.8 = f32[64,8,256]{2,1,0:T(8,128)} copy(f32[64,8,256]{2,1,0:T(8,128)} %shard_map.64) | data formatting | bytes 1048576

commit v3 on v2

--- a/solution.py
+++ b/solution.py
@@ -335,12 +335,7 @@
     @pl.loop(0, local // SUB)
     def _(block):
         span = pl.ds(pl.multiple_of(block * SUB, SUB), SUB)
-        state[span] = jnp.swapaxes(adv[:, span], 0, 1)
-        out_copy(block).start()
-
-    @pl.loop(0, local // SUB)
-    def _(block):
-        out_copy(block).wait()
+        out[span] = jnp.swapaxes(adv[:, span], 0, 1)
 
     for d in range(2):
         cell_copy(d).wait_send()
@@ -371,9 +366,9 @@
     dma = pltpu.SemaphoreType.DMA
     return pl.pallas_call(
         functools.partial(kernel, (n_band, n_mem, local, band_rows, lon, obs_rows, halves)),
-        out_shape=jax.ShapeDtypeStruct(state.shape, f32),
+        out_shape=pltpu.VMEM(state.shape, f32),
         in_specs=[pl.BlockSpec(memory_space=pltpu.HBM)] * 6,
-        out_specs=pl.BlockSpec(memory_space=pltpu.HBM),
+        out_specs=pl.BlockSpec(memory_space=pltpu.VMEM),
         scratch_shapes=[
             pltpu.VMEM(state.shape, f32),
             pltpu.VMEM(courant.shape, f32),
@@ -409,7 +404,7 @@
             dma((local // SUB,)),
         ],
         compiler_params=pltpu.CompilerParams(
-            collective_id=0, has_side_effects=True, vmem_limit_bytes=62 * 1024 * 1024
+            collective_id=0, has_side_effects=True, vmem_limit_bytes=60 * 1024 * 1024
         ),
     )(state, courant, obs_cell, block_rows, band_list, obs_pert)
 

time: 33.7 us -> 32 us (0.950)
  local copies, waits for them, and re-layouts: 1.87 us -> 0.8 us
  Pallas kernels: 31.7 us -> 31 us
    unnamed x1, local copies, waits for them, and re-layouts: 1.87 us -> 0.8 us
    pallas_call x1, Pallas kernels: 31.7 us -> 31 us  [shards(): pl.pallas_call(functools.partial(kernel, (n_band, n_mem, local, band_rows...]
where the time goes in v3:
time: 32 us; the launch traced here: 31.9 us
  Pallas kernels  31 us (97%)
  local copies, waits for them, and re-layouts  0.8 us (2%)
    pallas_call x1, Pallas kernels, shards(): pl.pallas_call(functools.partial(kernel, (n_band, n_mem, local, band_rows...  31 us
    unnamed x1, local copies, waits for them, and re-layouts  0.8 us

profile of v3, /device:TPU:0, one launch (start us, length us, event | category | flops | bytes accessed | tf_op | source)
XLA Modules:
  0.0 31.9 jit_solution(10554775325954417910)
XLA Ops:
  0.0 31.0 %shard_map.64 = f32[64,8,256]{2,1,0:T(8,128)S(1)} custom-call(f32[64,8,256]{2,1,0:T(8,128)} %state_in.1, f32[2,8,256]{2,1,0:T(8,128)} %courant_in.1, s32[1,512]{1,0:T(1,128)} %cells_in.1, s32[8]{0:T(128)} %rows_list.1, s32[1,2]{1,0:T(1,128)} %list_list.1, bf16[1,512,256]{2,1,0:T(8,128)(2,1)} %obs.1), custom_call_target="tpu_custom_call" | custom-call | tf_op jit(solution)/shard_map/pallas_call | solution.py:367
  31.1 0.8 %copy.8 = f32[64,8,256]{2,1,0:T(8,128)} copy(f32[64,8,256]{2,1,0:T(8,128)S(1)} %shard_map.64) | data formatting | bytes 1048576
